TPU v7x, 128 devices: a whole 4x4x4 slice. The times are simulated.
128 devices in a mesh: gx: 8 (over x_lo, y), gy: 4 (over z), gz: 4 (over x_hi, core).
Axes of the slice: x: 4 (x_hi: 2, x_lo: 2; x = x_hi * 2 + x_lo), y: 4, z: 4, core: 2. Of those that a mesh axis runs over, the one named last changes fastest.
Arguments:
- fields: float32 [5, 64, 512, 512], P(None, 'gz', 'gx', 'gy'), may hold values from -6 to 6
- metrics: float32 [2, 64, 512, 512], P(None, 'gz', 'gx', 'gy'), may hold values from 0.4 to 2.5
- jacobian_x: float32 [5, 5], replicated, may hold values from -2.5 to 2.5
- jacobian_y: float32 [5, 5], replicated, may hold values from -2.5 to 2.5
- pivot_inverse: bfloat16 [5, 5, 64, 512, 512], P(None, None, 'gz', 'gx', 'gy'), may hold values from -0.25 to 1.25, as said below
- lower_blocks: bfloat16 [5, 5, 64, 512, 512], P(None, None, 'gz', 'gx', 'gy'), may hold values from -1.3 to 0.1
- upper_blocks: bfloat16 [5, 5, 64, 512, 512], P(None, None, 'gz', 'gx', 'gy'), may hold values from -1 to 0.1
Outputs:
- new_fields: float32 [5, 64, 512, 512], P(None, 'gz', 'gx', 'gy')
Inputs may be any that keep to these rules, and one draw needn't show every extreme that they name: `pivot_inverse`: each 5x5 block is dominated by its diagonal.
All inputs are finite; a program needn't handle non-finite values.
Results may differ from a plain program's by a relative error of at most 0.0003.
Values sent between devices are 32-bit elements; how exact they have to be, the bound alone decides.
A program may use at most 128 MiB of HBM per device.

v0:
```python
import jax
import jax.numpy as jnp
from jax import lax
from jax.sharding import PartitionSpec as P

STEP = 0.25


def with_halo(block, sides, width):
    for axis, dim in sides:
        count = lax.axis_size(axis)
        forward = [(i, i + 1) for i in range(count - 1)]
        backward = [(target, source) for source, target in forward]
        low = lax.ppermute(
            lax.slice_in_dim(block, block.shape[dim] - width, None, axis=dim), axis, forward
        )
        high = lax.ppermute(lax.slice_in_dim(block, 0, width, axis=dim), axis, backward)
        block = jnp.concatenate([low, block, high], axis=dim)
    return block


def shifted(block, axis, distance):
    devices = range(lax.axis_size(axis))
    route = [(i - distance, i) for i in devices if i - distance in devices]
    return lax.ppermute(block, axis, route)


def apply_block(matrix, vector):
    return jnp.stack([sum((matrix[i][j] * vector[j] for j in range(5))) for i in range(5)])


def fourth_diff(padded, axis):
    number = padded.shape[axis] - 4

    def plane(start):
        return lax.slice_in_dim(padded, start, start + number, axis=axis)

    return (plane(0) - plane(4) + 8.0 * (plane(3) - plane(1))) / 12.0


def local(fields, metrics, jacobian_x, jacobian_y, pivot_inverse, lower_blocks, upper_blocks):
    depth = fields.shape[1]
    rows_x = fields.shape[2]
    rows_y = fields.shape[3]
    joined = jnp.concatenate([fields, metrics], 0)
    widened_field = with_halo(joined, (("gx", 2), ("gy", 3)), 2)
    along_x = widened_field[:, :, :, 2 : rows_y + 2]
    along_y = widened_field[:, :, 2 : rows_x + 2, :]
    x_padded_field = along_x[5] * apply_block(jacobian_x, along_x[:5])
    padded_y = along_y[6] * apply_block(jacobian_y, along_y[:5])
    forcing = -STEP * (fourth_diff(x_padded_field, 2) + fourth_diff(padded_y, 3))
    indices = jnp.arange(depth, dtype=jnp.int32)
    zero_plane = jnp.zeros((5, rows_x, rows_y), jnp.float32)

    def blocks_located(blocks, plane):
        return lax.dynamic_index_in_dim(blocks, plane, 2, keepdims=False).astype(jnp.float32)

    def elimination_downward(incoming_carry):

        def advance(carried, plane):
            source = lax.dynamic_index_in_dim(forcing, plane, 1, keepdims=False)
            result = apply_block(
                blocks_located(pivot_inverse, plane),
                source - apply_block(blocks_located(lower_blocks, plane), carried),
            )
            return (result, result)

        return lax.scan(advance, incoming_carry, indices)[1]

    def substitution_upward(forward_planes, incoming_carry):

        def retreat(carried, plane):
            source = lax.dynamic_index_in_dim(forward_planes, plane, 0, keepdims=False)
            result = source - apply_block(blocks_located(upper_blocks, plane), carried)
            return (result, result)

        return lax.scan(retreat, incoming_carry, indices, reverse=True)[1]

    carried = zero_plane
    for sweep_turn in range(lax.axis_size("gz") - 1):
        forward_planes = elimination_downward(carried)
        carried = shifted(forward_planes[-1], "gz", 1)
    forward_planes = elimination_downward(carried)
    carried = zero_plane
    for sweep_turn in range(lax.axis_size("gz") - 1):
        update_planes = substitution_upward(forward_planes, carried)
        carried = shifted(update_planes[0], "gz", -1)
    update_planes = substitution_upward(forward_planes, carried)
    return fields + jnp.transpose(update_planes, (1, 0, 2, 3))


def solution(mesh):
    placed = (
        P(None, "gz", "gx", "gy"),
        P(None, "gz", "gx", "gy"),
        P(),
        P(),
        P(None, None, "gz", "gx", "gy"),
        P(None, None, "gz", "gx", "gy"),
        P(None, None, "gz", "gx", "gy"),
    )
    return jax.shard_map(
        local, mesh=mesh, in_specs=placed, out_specs=P(None, "gz", "gx", "gy"), check_vma=False
    )
```

profile of v0, /device:TPU:1, one launch (start us, length us, event | category | flops | bytes accessed | tf_op | source)
XLA Modules:
  0.0 790.3 jit_solution(16333113946206305397)
XLA Ops:
  0.0 3.4 copy_dynamic-update-slice_fusion
  4.0 1.8 copy-done.2
  5.9 4.3 collective-permute-start
  13.6 4.3 copy.48
  17.9 4.4 copy.50
  23.0 2.4 pad_maximum_fusion
  25.4 4.5 fusion.606
  29.9 3.0 copy.44
  32.9 3.5 collective-permute-start.2
  36.4 3.0 copy.45
  39.4 1.7 collective-permute-start.3
  41.2 5.3 slice_bitcast_fusion.300
  46.4 3.2 add_dynamic-update-slice_fusion.8
  49.7 3.4 add_dynamic-update-slice_fusion.7
  53.1 3.4 add_dynamic-update-slice_fusion.6
  56.5 3.4 add_dynamic-update-slice_fusion.5
  60.1 2.9 copy.46
  63.0 2.8 copy.47
  65.8 7.7 add_dynamic-update-slice_fusion.4
  73.5 3.7 add_dynamic-update-slice_fusion.3
  77.2 3.8 add_dynamic-update-slice_fusion.2
  81.0 4.7 add_dynamic-update-slice_fusion.1
  85.8 4.2 add_dynamic-update-slice_fusion
  91.4 2.3 fusion.583
  94.5 1.8 broadcast.61.clone.2
  96.3 76.9 %while.113 = (s32[]{:T(128)}, f32[5,64,128]{2,1,0:T(8,128)S(1)}, f32[16,5,64,128]{3,2,1,0:T(8,128)}, s32[16]{0:T(128)S(1)}, bf16[5,5,16,64,128]{4,3,1,0,2:T(8,12...) while((s32[]{:T(128)}, f32[5,64,128]{2,1,0:T(8,128)S(1)}, ...), condition=%wide.region_1.2_spmd, body=%wide.region_0.1_spmd.sunk | while | flops 1187843 | bytes 6881947 | solution.py:68
  98.8 1.3 bitcast_convert_fusion.20
  103.6 1.3 bitcast_convert_fusion.20
  108.5 1.3 bitcast_convert_fusion.20
  113.3 1.3 bitcast_convert_fusion.20
  118.1 1.3 bitcast_convert_fusion.20
  122.9 1.3 bitcast_convert_fusion.20
  127.7 1.3 bitcast_convert_fusion.20
  132.5 1.3 bitcast_convert_fusion.20
  137.3 1.3 bitcast_convert_fusion.20
  142.1 1.3 bitcast_convert_fusion.20
  146.9 1.3 bitcast_convert_fusion.20
  156.5 1.3 bitcast_convert_fusion.20
  174.2 5.8 collective-permute-start.4
  180.0 2.2 collective-permute-done.4
  182.2 1.8 broadcast.61.clone.3
  184.0 76.9 %while.114 = (s32[]{:T(128)}, f32[5,64,128]{2,1,0:T(8,128)S(1)}, f32[16,5,64,128]{3,2,1,0:T(8,128)}, s32[16]{0:T(128)S(1)}, bf16[5,5,16,64,128]{4,3,1,0,2:T(8,12...) while((s32[]{:T(128)}, f32[5,64,128]{2,1,0:T(8,128)S(1)}, ...), condition=%wide.region_3.4_spmd, body=%wide.region_2.3_spmd.sunk | while | flops 1187843 | bytes 6881947 | solution.py:68
  261.9 5.9 collective-permute-start.5
  267.8 2.2 collective-permute-done.5
  270.0 1.8 broadcast.61.clone.4
  271.8 76.9 %while.115 = (s32[]{:T(128)}, f32[5,64,128]{2,1,0:T(8,128)S(1)}, f32[16,5,64,128]{3,2,1,0:T(8,128)}, s32[16]{0:T(128)S(1)}, bf16[5,5,16,64,128]{4,3,1,0,2:T(8,12...) while((s32[]{:T(128)}, f32[5,64,128]{2,1,0:T(8,128)S(1)}, ...), condition=%wide.region_5.6_spmd, body=%wide.region_4.5_spmd.sunk | while | flops 1187843 | bytes 6881947 | solution.py:68
  349.8 6.1 collective-permute-start.6
  356.0 7.2 copy.60
  363.5 85.0 %while.116 = (s32[]{:T(128)}, f32[5,64,128]{2,1,0:T(8,128)S(1)}, f32[16,5,64,128]{3,2,1,0:T(8,128)S(1)}, s32[16]{0:T(128)S(1)}, bf16[5,5,16,64,128]{4,3,1,0,2:T(...) while((s32[]{:T(128)}, f32[5,64,128]{2,1,0:T(8,128)S(1)}, ...), condition=%wide.region_7.8_spmd, body=%wide.region_6.7_spmd.sunk | while | flops 1187843 | bytes 6881439 | solution.py:68
  448.5 1.8 broadcast.61.clone.1
  450.3 97.0 %while.120 = (s32[]{:T(128)}, f32[5,64,128]{2,1,0:T(8,128)}, f32[16,5,64,128]{3,2,1,0:T(8,128)}, s32[16]{0:T(128)S(1)}, f32[16,5,64,128]{3,2,1,0:T(8,128)S(1)}, ...) while((s32[]{:T(128)}, f32[5,64,128]{2,1,0:T(8,128)}, ...), condition=%wide.region_9.10_spmd.clone, body=%wide.region_8.9_spmd.clone.sunk | while | flops 696326 | bytes 4833465 | solution.py:77
  548.3 1.9 collective-permute-start.7
  550.2 6.2 collective-permute-done.7
  556.4 1.8 broadcast.61.clone.6
  558.2 68.5 %while.117 = (s32[]{:T(128)}, f32[5,64,128]{2,1,0:T(8,128)S(1)}, f32[16,5,64,128]{3,2,1,0:T(8,128)}, s32[16]{0:T(128)S(1)}, f32[16,5,64,128]{3,2,1,0:T(8,128)S(1...) while((s32[]{:T(128)}, f32[5,64,128]{2,1,0:T(8,128)S(1)}, ...), condition=%wide.region_11.12_spmd, body=%wide.region_10.11_spmd.sunk | while | flops 655365 | bytes 4505775 | solution.py:77
  627.7 1.9 collective-permute-start.8
  629.6 6.2 collective-permute-done.8
  635.8 1.8 broadcast.61
  637.6 68.5 %while.118 = (s32[]{:T(128)}, f32[5,64,128]{2,1,0:T(8,128)S(1)}, f32[16,5,64,128]{3,2,1,0:T(8,128)}, s32[16]{0:T(128)S(1)}, f32[16,5,64,128]{3,2,1,0:T(8,128)S(1...) while((s32[]{:T(128)}, f32[5,64,128]{2,1,0:T(8,128)S(1)}, ...), condition=%wide.region_13.14_spmd, body=%wide.region_12.13_spmd.sunk | while | flops 655365 | bytes 4505775 | solution.py:77
  707.1 1.9 collective-permute-start.9
  709.0 6.2 collective-permute-done.9
  715.2 1.8 broadcast.61.clone
  717.0 68.5 %while.119 = (s32[]{:T(128)}, f32[5,64,128]{2,1,0:T(8,128)S(1)}, f32[16,5,64,128]{3,2,0,1:T(8,128)}, s32[16]{0:T(128)S(1)}, f32[16,5,64,128]{3,2,1,0:T(8,128)S(1...) while((s32[]{:T(128)}, f32[5,64,128]{2,1,0:T(8,128)S(1)}, ...), condition=%wide.region_15.16_spmd, body=%wide.region_14.15_spmd.sunk | while | flops 655365 | bytes 4505775 | solution.py:77
  785.5 4.8 bitcast_add_fusion
  (1855 shorter events, 372.1 us)
Async XLA Ops:
  0.0 3.4 copy-start.8
  0.0 11.5 %copy-start.9 = (f32[5,5]{1,0:T(8,128)S(1)}, f32[5,5]{1,0:T(8,128)}, u32[]{:S(2)}) copy-start(f32[5,5]{1,0:T(8,128)} %param.25) | copy-start | bytes 304
  0.0 12.9 %copy-start.10 = (f32[5,5]{1,0:T(8,128)S(1)}, f32[5,5]{1,0:T(8,128)}, u32[]{:S(2)}) copy-start(f32[5,5]{1,0:T(8,128)} %param.26) | copy-start | bytes 304
  0.0 13.6 %copy-start.7 = (bf16[5,5,16,64,128]{4,3,2,1,0:T(8,128)(2,1)S(1)}, bf16[5,5,16,64,128]{4,3,2,1,0:T(8,128)(2,1)}, u32[]{:S(2)}) copy-start(bf16[5,5,16,64,128]{4,3,2,1,0:T(8,128)(2,1)} %param.27) | copy-start | bytes 19660804
  4.0 1.8 copy-start.2
  5.8 12.0 %slice-start = ((s8[6553600]{0:T(1024)(128)(4,1)}), s8[4194304]{0:T(1024)(128)(4,1)S(1)}, s32[]{:S(2)}) async-start(s8[6553600]{0:T(1024)(128)(4,1)} %bitcast.3016), calls=%async_computation | async-start | bytes 8388608
  5.9 17.1 %collective-permute-start = (f32[7,16,2,128]{3,1,2,0:T(8,128)S(1)}, f32[7,16,2,128]{3,1,2,0:T(8,128)S(1)}, u32[]{:S(2)}, u32[]{:S(2)}) collective-permute-start(f32[7,16,2,128]{3,1,2,0:T(8,128)S(1)} %get-tuple-element.988), channel_id=1, source_target_pairs={{0,16},{16,32},{32,48},{48,64},{64,80},{80,96},{96,112},{1,17},{17... | collective-permute-start | bytes 344072 | tf_op jit(solution)/shard_map/ppermute | solution.py:14
  10.2 12.8 %collective-permute-start.1 = (f32[7,16,2,128]{3,1,2,0:T(8,128)S(1)}, f32[7,16,2,128]{3,1,2,0:T(8,128)S(1)}, u32[]{:S(2)}, u32[]{:S(2)}) collective-permute-start(f32[7,16,2,128]{3,1,2,0:T(8,128)S(1)} %get-tuple-element.989), channel_id=1, source_target_pairs={{16,0},{32,16},{48,32},{64,48},{80,64},{96,80},{112,96},{17,1},{33... | collective-permute-start | bytes 344072 | tf_op jit(solution)/shard_map/ppermute | solution.py:17
  13.6 4.3 slice-start.1
  25.4 4.5 copy-start
  32.9 27.2 %collective-permute-start.2 = (f32[7,16,68,2]{2,1,3,0:T(8,128)S(1)}, f32[7,16,68,2]{2,1,3,0:T(8,128)S(1)}, u32[]{:S(2)}, u32[]{:S(2)}) collective-permute-start(f32[7,16,68,2]{2,1,3,0:T(8,128)S(1)} %copy.44), channel_id=1, source_target_pairs={{0,4},{4,8},{8,12},{1,5},{5,9},{9,13},{2,6},{6,10},{10,14},{3,7},{... | collective-permute-start | bytes 182792 | tf_op jit(solution)/shard_map/ppermute | solution.py:14
  39.4 7.0 copy-start.1
  39.4 23.6 %collective-permute-start.3 = (f32[7,16,68,2]{2,1,3,0:T(8,128)S(1)}, f32[7,16,68,2]{2,1,3,0:T(8,128)S(1)}, u32[]{:S(2)}, u32[]{:S(2)}) collective-permute-start(f32[7,16,68,2]{2,1,3,0:T(8,128)S(1)} %copy.45), channel_id=1, source_target_pairs={{4,0},{8,4},{12,8},{5,1},{9,5},{13,9},{6,2},{10,6},{14,10},{7,3},{... | collective-permute-start | bytes 182792 | tf_op jit(solution)/shard_map/ppermute | solution.py:17
  81.0 8.9 %copy-start.4 = (f32[7,16,68,2]{3,1,2,0:T(8,128)S(1)}, f32[7,16,68,2]{3,1,2,0:T(8,128)}, u32[]{:S(2)}) copy-start(f32[7,16,68,2]{3,1,2,0:T(8,128)} %copy.46) | copy-start | bytes 182788
  81.0 8.9 %copy-start.5 = (f32[7,16,68,2]{3,1,2,0:T(8,128)S(1)}, f32[7,16,68,2]{3,1,2,0:T(8,128)}, u32[]{:S(2)}) copy-start(f32[7,16,68,2]{3,1,2,0:T(8,128)} %copy.47) | copy-start | bytes 182788
  85.7 4.2 copy-start.3
  174.2 8.0 %collective-permute-start.4 = (f32[5,64,128]{2,1,0:T(8,128)S(1)}, f32[5,64,128]{2,1,0:T(8,128)S(1)}, u32[]{:S(2)}, u32[]{:S(2)}) collective-permute-start(f32[5,64,128]{2,1,0:T(8,128)S(1)} %slice_bitcast_fusion.306), channel_id=1, source_target_pairs={{0,1},{1,2},{2,3},{4,5},{5,6},{6,7},{8,9},{9,10},{10,11},{12,13},{... | collective-permute-start | bytes 491528 | tf_op jit(solution)/shard_map/ppermute | solution.py:25
  261.9 8.1 %collective-permute-start.5 = (f32[5,64,128]{2,1,0:T(8,128)S(1)}, f32[5,64,128]{2,1,0:T(8,128)S(1)}, u32[]{:S(2)}, u32[]{:S(2)}) collective-permute-start(f32[5,64,128]{2,1,0:T(8,128)S(1)} %slice_bitcast_fusion.305), channel_id=1, source_target_pairs={{0,1},{1,2},{2,3},{4,5},{5,6},{6,7},{8,9},{9,10},{10,11},{12,13},{... | collective-permute-start | bytes 491528 | tf_op jit(solution)/shard_map/ppermute | solution.py:25
  348.7 14.4 %copy-start.6 = (f32[5,16,64,128]{3,2,0,1:T(8,128)}, f32[5,16,64,128]{3,2,0,1:T(8,128)S(1)}, u32[]{:S(2)}) copy-start(f32[5,16,64,128]{3,2,0,1:T(8,128)S(1)} %get-tuple-element.1716) | copy-start | bytes 7864324
  349.8 13.3 %collective-permute-start.6 = (f32[5,64,128]{2,1,0:T(8,128)S(1)}, f32[5,64,128]{2,1,0:T(8,128)S(1)}, u32[]{:S(2)}, u32[]{:S(2)}) collective-permute-start(f32[5,64,128]{2,1,0:T(8,128)S(1)} %slice_bitcast_fusion.304), channel_id=1, source_target_pairs={{0,1},{1,2},{2,3},{4,5},{5,6},{6,7},{8,9},{9,10},{10,11},{12,13},{... | collective-permute-start | bytes 491528 | tf_op jit(solution)/shard_map/ppermute | solution.py:25
  548.3 8.1 %collective-permute-start.7 = (f32[5,64,128]{2,1,0:T(8,128)S(1)}, f32[5,64,128]{2,1,0:T(8,128)S(1)}, u32[]{:S(2)}, u32[]{:S(2)}) collective-permute-start(f32[5,64,128]{2,1,0:T(8,128)S(1)} %slice_bitcast_fusion.303), channel_id=1, source_target_pairs={{1,0},{2,1},{3,2},{5,4},{6,5},{7,6},{9,8},{10,9},{11,10},{13,12},{... | collective-permute-start | bytes 491528 | tf_op jit(solution)/shard_map/ppermute | solution.py:25
  627.7 8.1 %collective-permute-start.8 = (f32[5,64,128]{2,1,0:T(8,128)S(1)}, f32[5,64,128]{2,1,0:T(8,128)S(1)}, u32[]{:S(2)}, u32[]{:S(2)}) collective-permute-start(f32[5,64,128]{2,1,0:T(8,128)S(1)} %slice_bitcast_fusion.302), channel_id=1, source_target_pairs={{1,0},{2,1},{3,2},{5,4},{6,5},{7,6},{9,8},{10,9},{11,10},{13,12},{... | collective-permute-start | bytes 491528 | tf_op jit(solution)/shard_map/ppermute | solution.py:25
  707.1 8.1 %collective-permute-start.9 = (f32[5,64,128]{2,1,0:T(8,128)S(1)}, f32[5,64,128]{2,1,0:T(8,128)S(1)}, u32[]{:S(2)}, u32[]{:S(2)}) collective-permute-start(f32[5,64,128]{2,1,0:T(8,128)S(1)} %slice_bitcast_fusion.301), channel_id=1, source_target_pairs={{1,0},{2,1},{3,2},{5,4},{6,5},{7,6},{9,8},{10,9},{11,10},{13,12},{... | collective-permute-start | bytes 491528 | tf_op jit(solution)/shard_map/ppermute | solution.py:25
where the time goes:
time: 801 us; the launch traced here: 790 us
  other arithmetic  314 us (39%)
  loops' own time  244 us (30%)
  local copies, waits for them, and re-layouts  174 us (22%)
  starting transfers between devices  34.4 us (4%)
  waiting for transfers between devices  23.1 us (3%)
    convert_element_type x128, other arithmetic, blocks_located(): lax.dynamic_index_in_dim(blocks, plane, 2, keepdims=False)  153 us
    another operation x4, loops' own time, elimination_downward(): return lax.scan(advance, incoming_carry, indices)[1]  127 us
    another operation x4, loops' own time, substitution_upward(): return lax.scan(retreat, incoming_carry, indices, reverse=True)[1]  116 us
    dynamic_slice x128, local copies, waits for them, and re-layouts, elimination_downward(): return lax.scan(advance, incoming_carry, indices)[1]  79.5 us
    dynamic_update_slice x64, other arithmetic, elimination_downward(): return lax.scan(advance, incoming_carry, indices)[1]  44.5 us
    dynamic_update_slice x64, local copies, waits for them, and re-layouts, elimination_downward(): return lax.scan(advance, incoming_carry, indices)[1]  33.2 us
    while x784, other arithmetic  30.9 us
    unnamed x9, other arithmetic  30 us
  transfers between devices with their start and end apart: 10, of which 5 were waited for; matrix products, arithmetic and copies ran while one was open for 5% of the time, Pallas kernels for 0%

commit v1 on v0

v1 whole, which is shorter than its diff:
```python
import jax
import jax.numpy as jnp
from jax import lax
from jax.experimental import pallas as pl
from jax.experimental.pallas import tpu as pltpu
from jax.sharding import PartitionSpec as P

STEP = 0.25
SCALE = -STEP / 12.0
CHUNK = 16
LANES = 128
F32 = jnp.float32
BF16 = jnp.bfloat16


def sum_of(terms):
    total = terms[0]
    for term in terms[1:]:
        total = total + term
    return total


def kernel(
    fields, metrics, jx, jy, pivot, lower, upper, out,
    cells, pv, lo, up, fx, w, result, band,
    xsend, xrecv, ysend, yrecv, corr, up_send, up_recv, down_send, down_recv,
    cell_sem, block_sem, out_sem, halo_ssem, halo_rsem, up_ssem, up_rsem, down_ssem, down_rsem,
):
    depth, rows = fields.shape[1], fields.shape[2]
    chunks = rows // CHUNK
    gx, gy, gz = lax.axis_index("gx"), lax.axis_index("gy"), lax.axis_index("gz")
    nx, ny, nz = lax.axis_size("gx"), lax.axis_size("gy"), lax.axis_size("gz")

    cell_copies = []
    for v in range(7):
        source = fields.at[v] if v < 5 else metrics.at[v - 5]
        cell_copies.append(pltpu.make_async_copy(source, cells.at[v], cell_sem.at[v]))
    for copy in cell_copies:
        copy.start()
    block_copies = {}
    for kind, (source, target) in enumerate(((lower, lo), (pivot, pv), (upper, up))):
        for c in range(chunks):
            part = pl.ds(c * CHUNK, CHUNK)
            block_copies[kind, c] = pltpu.make_async_copy(
                source.at[:, :, :, part, :], target.at[:, :, :, part, :], block_sem.at[kind, c]
            )
    for c in range(chunks):
        block_copies[0, c].start()
        block_copies[1, c].start()
    for c in range(chunks):
        block_copies[2, c].start()

    barrier = pltpu.get_barrier_semaphore()
    number = jnp.int32(0)
    for axis, place, size in (("gx", gx, nx), ("gy", gy, ny), ("gz", gz, nz)):
        @pl.when(place > 0)
        def _():
            pl.semaphore_signal(barrier, inc=1, device_id={axis: place - 1}, device_id_type=pl.DeviceIdType.MESH)

        @pl.when(place < size - 1)
        def _():
            pl.semaphore_signal(barrier, inc=1, device_id={axis: place + 1}, device_id_type=pl.DeviceIdType.MESH)

        number = number + jnp.where(place > 0, 1, 0) + jnp.where(place < size - 1, 1, 0)

    def halo_copy(which, target):
        source, destination = ((xsend, xrecv), (ysend, yrecv))[which // 2]
        axis = ("gx", "gy")[which // 2]
        return pltpu.make_async_remote_copy(
            src_ref=source.at[which % 2], dst_ref=destination.at[which % 2],
            send_sem=halo_ssem.at[which], recv_sem=halo_rsem.at[which],
            device_id={axis: target}, device_id_type=pl.DeviceIdType.MESH,
        )

    halos = []
    for which, (place, size) in enumerate(((gx, nx), (gx, nx), (gy, ny), (gy, ny))):
        upward = which % 2 == 0
        copy = halo_copy(which, place + 1 if upward else place - 1)
        sends = place < size - 1 if upward else place > 0
        receives = place > 0 if upward else place < size - 1
        halos.append((copy, sends, receives))

    def up_copy(c):
        return pltpu.make_async_remote_copy(
            src_ref=up_send.at[c], dst_ref=up_recv.at[c], send_sem=up_ssem.at[c], recv_sem=up_rsem.at[c],
            device_id={"gz": gz + 1}, device_id_type=pl.DeviceIdType.MESH,
        )

    def down_copy(c):
        return pltpu.make_async_remote_copy(
            src_ref=down_send.at[c], dst_ref=down_recv.at[c], send_sem=down_ssem.at[c], recv_sem=down_rsem.at[c],
            device_id={"gz": gz - 1}, device_id_type=pl.DeviceIdType.MESH,
        )

    @pl.when(gx == 0)
    def _():
        xrecv[0] = jnp.zeros(xrecv.shape[1:], F32)

    @pl.when(gx == nx - 1)
    def _():
        xrecv[1] = jnp.zeros(xrecv.shape[1:], F32)

    @pl.when(gy == 0)
    def _():
        yrecv[0] = jnp.zeros(yrecv.shape[1:], F32)

    @pl.when(gy == ny - 1)
    def _():
        yrecv[1] = jnp.zeros(yrecv.shape[1:], F32)

    @pl.when(gz == 0)
    def _():
        up_recv[...] = jnp.zeros(up_recv.shape, F32)

    @pl.when(gz == nz - 1)
    def _():
        down_recv[...] = jnp.zeros(down_recv.shape, F32)

    k = lax.broadcasted_iota(jnp.int32, (2 * LANES, LANES), 0)
    j = lax.broadcasted_iota(jnp.int32, (2 * LANES, LANES), 1)
    d = (j - k) & (LANES - 1)
    weight = jnp.where(d == 2, 1.0, 0.0) - jnp.where(d == LANES - 2, 1.0, 0.0)
    weight = weight + jnp.where(d == LANES - 1, 8.0, 0.0) - jnp.where(d == 1, 8.0, 0.0)
    band[...] = weight.astype(BF16)

    for copy in cell_copies:
        copy.wait()

    def pack_x(v, carry):
        for z in range(depth):
            xsend[0, v, 2 * z : 2 * z + 2, :] = cells[v, z, rows - 2 : rows, :]
            xsend[1, v, 2 * z : 2 * z + 2, :] = cells[v, z, 0:2, :]
        return carry

    lax.fori_loop(0, 6, pack_x, 0)
    pl.semaphore_wait(barrier, number)
    for which in (0, 1):
        copy, sends, _ = halos[which]
        pl.when(sends)(copy.start)

    lane = lax.broadcasted_iota(jnp.int32, (CHUNK, LANES), 1)
    pair = lane >> 1

    def pack_y(v, carry):
        low = jnp.zeros((CHUNK, LANES), F32)
        high = low
        for c in range(chunks):
            for z in range(depth):
                slot = CHUNK * c + z
                rolled = cells[v + v // 5, z, c * CHUNK : (c + 1) * CHUNK, :]
                if slot:
                    rolled = pltpu.roll(rolled, 2 * slot, 1)
                low = jnp.where(pair == slot, rolled, low)
                high = jnp.where(pair == (slot - 1) % (LANES // 2), rolled, high)
        ysend[0, v] = high
        ysend[1, v] = low
        return carry

    lax.fori_loop(0, 6, pack_y, 0)
    for which in (2, 3):
        copy, sends, _ = halos[which]
        pl.when(sends)(copy.start)

    jacobian_x = [[jx[i, j] for j in range(5)] for i in range(5)]
    jacobian_y = [[jy[i, j] for j in range(5)] for i in range(5)]

    def flux(jacobian, values, metric):
        factor = metric * SCALE
        return [factor * sum_of([jacobian[i][j] * values[j] for j in range(5)]) for i in range(5)]

    def x_plane(z, carry):
        for c in range(chunks):
            part = pl.ds(c * CHUNK, CHUNK)
            values = flux(jacobian_x, [cells[j, z, part, :] for j in range(5)], cells[5, z, part, :])
            for i in range(5):
                fx[i, z, 8 + c * CHUNK : 8 + (c + 1) * CHUNK, :] = values[i]
        return carry

    lax.fori_loop(0, depth, x_plane, 0)

    def y_plane(z, carry):
        stacks = []
        for c in range(chunks):
            part = pl.ds(c * CHUNK, CHUNK)
            values = flux(jacobian_y, [cells[j, z, part, :] for j in range(5)], cells[6, z, part, :])
            for value in values:
                first = value.astype(BF16)
                second = (value - first.astype(F32)).astype(BF16)
                stacks.append(jnp.concatenate([first, second], 1))
        product = jnp.dot(jnp.concatenate(stacks, 0), band[...], preferred_element_type=F32)
        for c in range(chunks):
            for i in range(5):
                at = (c * 5 + i) * CHUNK
                w[i, z, c * CHUNK : (c + 1) * CHUNK, :] = product[at : at + CHUNK, :]
        return carry

    lax.fori_loop(0, depth, y_plane, 0)

    for copy, _, receives in halos:
        pl.when(receives)(copy.wait_recv)

    for side in range(2):
        values = flux(jacobian_x, [xrecv[side, j] for j in range(5)], xrecv[side, 5])
        for i in range(5):
            for z in range(depth):
                start = 6 if side == 0 else 8 + rows
                fx[i, z, start : start + 2, :] = values[i][2 * z : 2 * z + 2, :]

    theirs = [flux(jacobian_y, [yrecv[s, j] for j in range(5)], yrecv[s, 5]) for s in range(2)]
    mine = [flux(jacobian_y, [ysend[s, j] for j in range(5)], ysend[s, 5]) for s in range(2)]
    odd = (lane & 1) == 1
    upper_pair = (lane & 2) == 2
    for i in range(5):
        high = theirs[0][i] - mine[0][i]
        low = theirs[1][i] - mine[1][i]
        at_start = high - jnp.where(odd, 0.0, 8.0 * pltpu.roll(high, LANES - 1, 1))
        at_end = jnp.where(odd, 8.0 * pltpu.roll(low, 1, 1), 0.0) - low
        at_end = pltpu.roll(at_end, LANES - 4, 1)
        corr[0, i] = jnp.where(upper_pair, at_start, at_end)
        corr[1, i] = jnp.where(upper_pair, at_end, at_start)

    edge = (lane < 2) | (lane >= LANES - 2)

    def force(c):
        base = 8 + c * CHUNK

        def plane(z, carry):
            shift = (2 + 2 * LANES - 2 * CHUNK * c - 2 * z) & (LANES - 1)
            for i in range(5):
                below2 = fx[i, z, base - 2 : base - 2 + CHUNK, :]
                below1 = fx[i, z, base - 1 : base - 1 + CHUNK, :]
                above1 = fx[i, z, base + 1 : base + 1 + CHUNK, :]
                above2 = fx[i, z, base + 2 : base + 2 + CHUNK, :]
                extra = jnp.where(edge, pltpu.roll(corr[z & 1, i], shift, 1), 0.0)
                at = (i, z, pl.ds(c * CHUNK, CHUNK), slice(None))
                w[at] = w[at] + extra + ((below2 - above2) + 8.0 * (above1 - below1))
            return carry

        lax.fori_loop(0, depth, plane, 0)

    def ahead(c):
        part = pl.ds(c * CHUNK, CHUNK)
        block_copies[0, c].wait()
        block_copies[1, c].wait()

        pl.when(gz > 0)(up_copy(c).wait_recv)

        def plane(z, carried):
            inner = []
            for i in range(5):
                total = w[i, z, part, :]
                for j in range(5):
                    total = total - lo[i, j, z, part, :].astype(F32) * carried[j]
                inner.append(total)
            result_here = []
            for i in range(5):
                total = sum_of([pv[i, j, z, part, :].astype(F32) * inner[j] for j in range(5)])
                w[i, z, part, :] = total
                result_here.append(total)
            return tuple(result_here)

        carried = lax.fori_loop(0, depth, plane, tuple(up_recv[c, i] for i in range(5)))
        for i in range(5):
            up_send[c, i] = carried[i]
        pl.when(gz < nz - 1)(up_copy(c).start)

    def out_copy(c):
        part = pl.ds(c * CHUNK, CHUNK)
        return pltpu.make_async_copy(result.at[:, :, part, :], out.at[:, :, part, :], out_sem.at[c])

    def back(c):
        part = pl.ds(c * CHUNK, CHUNK)
        pl.when(gz < nz - 1)(down_copy(c).wait_recv)

        def plane(step, carried):
            z = depth - 1 - step
            new = []
            for i in range(5):
                total = w[i, z, part, :]
                for j in range(5):
                    total = total - up[i, j, z, part, :].astype(F32) * carried[j]
                result[i, z, part, :] = cells[i, z, part, :] + total
                new.append(total)
            return tuple(new)

        carried = lax.fori_loop(0, depth, plane, tuple(down_recv[c, i] for i in range(5)))
        for i in range(5):
            down_send[c, i] = carried[i]
        pl.when(gz > 0)(down_copy(c).start)
        out_copy(c).start()

    @pl.when(gz > 0)
    def _():
        for c in range(chunks):
            force(c)

    for c in range(chunks):
        @pl.when(gz == 0)
        def _():
            force(c)

        ahead(c)

        @pl.when(gz == nz - 1)
        def _():
            block_copies[2, c].wait()
            back(c)

    @pl.when(gz < nz - 1)
    def _():
        for c in range(chunks):
            block_copies[2, c].wait()
            back(c)

    for c in range(chunks):
        out_copy(c).wait()
        pl.when(gz < nz - 1)(up_copy(c).wait_send)
        pl.when(gz > 0)(down_copy(c).wait_send)
    for copy, sends, _ in halos:
        pl.when(sends)(copy.wait_send)


def local(fields, metrics, jacobian_x, jacobian_y, pivot_inverse, lower_blocks, upper_blocks):
    _, depth, rows, columns = fields.shape
    chunks = rows // CHUNK
    anywhere = pl.BlockSpec(memory_space=pl.ANY)
    scalars = pl.BlockSpec(memory_space=pltpu.SMEM)
    dma = pltpu.SemaphoreType.DMA
    return pl.pallas_call(
        kernel,
        out_shape=jax.ShapeDtypeStruct(fields.shape, F32),
        in_specs=[anywhere, anywhere, scalars, scalars, anywhere, anywhere, anywhere],
        out_specs=anywhere,
        scratch_shapes=[
            pltpu.VMEM((7, depth, rows, columns), F32),
            pltpu.VMEM(pivot_inverse.shape, BF16),
            pltpu.VMEM(pivot_inverse.shape, BF16),
            pltpu.VMEM(pivot_inverse.shape, BF16),
            pltpu.VMEM((5, depth, rows + 16, columns), F32),
            pltpu.VMEM(fields.shape, F32),
            pltpu.VMEM(fields.shape, F32),
            pltpu.VMEM((2 * LANES, LANES), BF16),
            pltpu.VMEM((2, 6, 2 * depth, columns), F32),
            pltpu.VMEM((2, 6, 2 * depth, columns), F32),
            pltpu.VMEM((2, 6, CHUNK, LANES), F32),
            pltpu.VMEM((2, 6, CHUNK, LANES), F32),
            pltpu.VMEM((2, 5, CHUNK, LANES), F32),
            pltpu.VMEM((chunks, 5, CHUNK, LANES), F32),
            pltpu.VMEM((chunks, 5, CHUNK, LANES), F32),
            pltpu.VMEM((chunks, 5, CHUNK, LANES), F32),
            pltpu.VMEM((chunks, 5, CHUNK, LANES), F32),
            dma((7,)),
            dma((3, chunks)),
            dma((chunks,)),
            dma((4,)),
            dma((4,)),
            dma((chunks,)),
            dma((chunks,)),
            dma((chunks,)),
            dma((chunks,)),
        ],
        compiler_params=pltpu.CompilerParams(
            collective_id=0, has_side_effects=True, vmem_limit_bytes=48 * 1024 * 1024
        ),
    )(fields, metrics, jacobian_x, jacobian_y, pivot_inverse, lower_blocks, upper_blocks)


def solution(mesh):
    cells = P(None, "gz", "gx", "gy")
    blocks = P(None, None, "gz", "gx", "gy")
    return jax.shard_map(
        local, mesh=mesh, in_specs=(cells, cells, P(), P(), blocks, blocks, blocks),
        out_specs=cells, check_vma=False,
    )
```

time: 801 us -> 38.1 us (0.05); the launches traced: 790 us -> 37.9 us
  other arithmetic: 314 us -> 0 us
  loops' own time: 244 us -> 0 us
  local copies, waits for them, and re-layouts: 174 us -> 4.09 us
  starting transfers between devices: 34.4 us -> 0 us
  Pallas kernels: 0 us -> 33.8 us
  waiting for transfers between devices: 23.1 us -> 0 us
    another operation x8 -> x0, loops' own time: 244 us -> none  [the longest x4 127 us: elimination_downward(): return lax.scan(advance, incoming_carry, indices)[1]]
    convert_element_type x128 -> x0, other arithmetic: 153 us -> none  [blocks_located(): lax.dynamic_index_in_dim(blocks, plane, 2, keepdims=False)]
    dynamic_slice x128 -> x0, local copies, waits for them, and re-layouts: 79.5 us -> none  [elimination_downward(): return lax.scan(advance, incoming_carry, indices)[1]]
    dynamic_update_slice x64 -> x0, other arithmetic: 44.5 us -> none  [elimination_downward(): return lax.scan(advance, incoming_carry, indices)[1]]
    ppermute x10 -> x0, starting transfers between devices: 34.4 us -> none  [the longest x6 23.5 us: shifted(): return lax.ppermute(block, axis, route)]
    pallas_call x0 -> x1, Pallas kernels: none -> 33.8 us  [local(): pl.pallas_call(kernel, out_shape=jax.ShapeDtypeStruct(fields.shape, F32),...]
    dynamic_update_slice x64 -> x0, local copies, waits for them, and re-layouts: 33.2 us -> none  [elimination_downward(): return lax.scan(advance, incoming_carry, indices)[1]]
    while x784 -> x0, other arithmetic: 30.9 us -> none
  transfers between devices with their start and end apart: 10 -> 0, of which waited for: 5 -> 0; matrix products, arithmetic and copies ran while one was open for 5% -> 0% of each run, Pallas kernels for 0% -> 0%
where the time goes in v1:
time: 38.1 us; the launch traced here: 37.9 us
  Pallas kernels  33.8 us (89%)
  local copies, waits for them, and re-layouts  4.09 us (11%)
    pallas_call x1, Pallas kernels, local(): pl.pallas_call(kernel, out_shape=jax.ShapeDtypeStruct(fields.shape, F32),...  33.8 us
    unnamed x7, local copies, waits for them, and re-layouts  4.09 us

profile of v1, /device:TPU:1, one launch (start us, length us, event | category | flops | bytes accessed | tf_op | source)
XLA Modules:
  0.0 37.9 jit_solution(1981349032394642986)
XLA Ops:
  0.0 0.0 copy-start
  0.0 1.2 %copy-done = f32[2,16,64,128]{3,2,1,0:T(8,128)S(1)} copy-done((f32[2,16,64,128]{3,2,1,0:T(8,128)S(1)}, f32[2,16,64,128]{3,2,1,0:T(8,128)}, u32[]{:S(2)}) %copy-start) | copy-done | bytes 1048600
  1.2 0.0 copy-start.1
  1.2 0.7 %copy-done.1 = f32[5,5]{1,0:T(8,128)S(1)} copy-done((f32[5,5]{1,0:T(8,128)S(1)}, f32[5,5]{1,0:T(8,128)}, u32[]{:S(2)}) %copy-start.1) | copy-done | bytes 124
  1.9 0.0 copy-start.2
  1.9 0.7 %copy-done.2 = f32[5,5]{1,0:T(8,128)S(1)} copy-done((f32[5,5]{1,0:T(8,128)S(1)}, f32[5,5]{1,0:T(8,128)}, u32[]{:S(2)}) %copy-start.2) | copy-done | bytes 124
  2.6 33.8 %shard_map.73 = f32[5,16,64,128]{3,2,1,0:T(8,128)S(1)} custom-call(f32[5,16,64,128]{3,2,1,0:T(8,128)} %fields.1, f32[2,16,64,128]{3,2,1,0:T(8,128)S(1)} %copy-done, f32[5,5]{1,0:T(8,128)S(1)} %copy-done.1, f32[5,5]{1,0:T(8,128)S(1)} %copy-done.2, bf16[5,5,16,64,128]{4,3,2,1,0:T(8,128)(2,1)} %pivot.1, bf16[5,5,16,64,128]{4,3,2,1,0:T(8,128)(2,1)} %lower.1, ...), custom_call_target="tpu_custom_call" | custom-call | tf_op jit(solution)/shard_map/pallas_call | solution.py:329
  36.4 1.5 %copy.9 = f32[5,16,64,128]{3,2,1,0:T(8,128)} copy(f32[5,16,64,128]{3,2,1,0:T(8,128)S(1)} %shard_map.73) | data formatting | bytes 5242880
Async XLA Ops:
  0.0 1.2 %copy-start = (f32[2,16,64,128]{3,2,1,0:T(8,128)S(1)}, f32[2,16,64,128]{3,2,1,0:T(8,128)}, u32[]{:S(2)}) copy-start(f32[2,16,64,128]{3,2,1,0:T(8,128)} %metrics.1) | copy-start | bytes 3145732
  1.2 0.7 %copy-start.1 = (f32[5,5]{1,0:T(8,128)S(1)}, f32[5,5]{1,0:T(8,128)}, u32[]{:S(2)}) copy-start(f32[5,5]{1,0:T(8,128)} %jx.1) | copy-start | bytes 304
  1.9 0.7 %copy-start.2 = (f32[5,5]{1,0:T(8,128)S(1)}, f32[5,5]{1,0:T(8,128)}, u32[]{:S(2)}) copy-start(f32[5,5]{1,0:T(8,128)} %jy.1) | copy-start | bytes 304

commit v2 on v1

--- a/solution.py
+++ b/solution.py
@@ -11,6 +11,7 @@
 LANES = 128
 F32 = jnp.float32
 BF16 = jnp.bfloat16
+VMEM_LIMIT = 48 * 1024 * 1024
 
 
 def sum_of(terms):
@@ -21,17 +22,20 @@
 
 
 def kernel(
-    fields, metrics, jx, jy, pivot, lower, upper, out,
-    cells, pv, lo, up, fx, w, result, band,
+    fields, metrics, jacobian_x, jacobian_y, pivot, lower, upper, out,
+    jx, jy, cells, pv, lo, up, fx, w, result, band,
     xsend, xrecv, ysend, yrecv, corr, up_send, up_recv, down_send, down_recv,
-    cell_sem, block_sem, out_sem, halo_ssem, halo_rsem, up_ssem, up_rsem, down_ssem, down_rsem,
+    jacobian_sem, cell_sem, block_sem, out_sem, halo_ssem, halo_rsem, up_ssem, up_rsem, down_ssem, down_rsem,
 ):
     depth, rows = fields.shape[1], fields.shape[2]
     chunks = rows // CHUNK
     gx, gy, gz = lax.axis_index("gx"), lax.axis_index("gy"), lax.axis_index("gz")
     nx, ny, nz = lax.axis_size("gx"), lax.axis_size("gy"), lax.axis_size("gz")
 
-    cell_copies = []
+    cell_copies = [
+        pltpu.make_async_copy(jacobian_x, jx, jacobian_sem.at[0]),
+        pltpu.make_async_copy(jacobian_y, jy, jacobian_sem.at[1]),
+    ]
     for v in range(7):
         source = fields.at[v] if v < 5 else metrics.at[v - 5]
         cell_copies.append(pltpu.make_async_copy(source, cells.at[v], cell_sem.at[v]))
@@ -161,53 +165,58 @@
         copy, sends, _ = halos[which]
         pl.when(sends)(copy.start)
 
-    jacobian_x = [[jx[i, j] for j in range(5)] for i in range(5)]
-    jacobian_y = [[jy[i, j] for j in range(5)] for i in range(5)]
-
-    def flux(jacobian, values, metric):
+    matrix_x = [[jx[i, j] for j in range(5)] for i in range(5)]
+    matrix_y = [[jy[i, j] for j in range(5)] for i in range(5)]
+
+    def flux(matrix, values, metric):
         factor = metric * SCALE
-        return [factor * sum_of([jacobian[i][j] * values[j] for j in range(5)]) for i in range(5)]
+        return [factor * sum_of([matrix[i][j] * values[j] for j in range(5)]) for i in range(5)]
 
     def x_plane(z, carry):
         for c in range(chunks):
             part = pl.ds(c * CHUNK, CHUNK)
-            values = flux(jacobian_x, [cells[j, z, part, :] for j in range(5)], cells[5, z, part, :])
+            values = flux(matrix_x, [cells[j, z, part, :] for j in range(5)], cells[5, z, part, :])
             for i in range(5):
                 fx[i, z, 8 + c * CHUNK : 8 + (c + 1) * CHUNK, :] = values[i]
         return carry
 
     lax.fori_loop(0, depth, x_plane, 0)
 
-    def y_plane(z, carry):
+    group = min(8, depth)
+
+    def y_planes(step, carry):
         stacks = []
-        for c in range(chunks):
-            part = pl.ds(c * CHUNK, CHUNK)
-            values = flux(jacobian_y, [cells[j, z, part, :] for j in range(5)], cells[6, z, part, :])
-            for value in values:
-                first = value.astype(BF16)
-                second = (value - first.astype(F32)).astype(BF16)
-                stacks.append(jnp.concatenate([first, second], 1))
+        for z in range(group):
+            for c in range(chunks):
+                part = pl.ds(c * CHUNK, CHUNK)
+                at = step * group + z
+                values = flux(matrix_y, [cells[j, at, part, :] for j in range(5)], cells[6, at, part, :])
+                for value in values:
+                    first = value.astype(BF16)
+                    second = (value - first.astype(F32)).astype(BF16)
+                    stacks.append(jnp.concatenate([first, second], 1))
         product = jnp.dot(jnp.concatenate(stacks, 0), band[...], preferred_element_type=F32)
-        for c in range(chunks):
-            for i in range(5):
-                at = (c * 5 + i) * CHUNK
-                w[i, z, c * CHUNK : (c + 1) * CHUNK, :] = product[at : at + CHUNK, :]
+        for z in range(group):
+            for c in range(chunks):
+                for i in range(5):
+                    at = ((z * chunks + c) * 5 + i) * CHUNK
+                    w[i, step * group + z, c * CHUNK : (c + 1) * CHUNK, :] = product[at : at + CHUNK, :]
         return carry
 
-    lax.fori_loop(0, depth, y_plane, 0)
+    lax.fori_loop(0, depth // group, y_planes, 0)
 
     for copy, _, receives in halos:
         pl.when(receives)(copy.wait_recv)
 
     for side in range(2):
-        values = flux(jacobian_x, [xrecv[side, j] for j in range(5)], xrecv[side, 5])
+        values = flux(matrix_x, [xrecv[side, j] for j in range(5)], xrecv[side, 5])
         for i in range(5):
             for z in range(depth):
                 start = 6 if side == 0 else 8 + rows
                 fx[i, z, start : start + 2, :] = values[i][2 * z : 2 * z + 2, :]
 
-    theirs = [flux(jacobian_y, [yrecv[s, j] for j in range(5)], yrecv[s, 5]) for s in range(2)]
-    mine = [flux(jacobian_y, [ysend[s, j] for j in range(5)], ysend[s, 5]) for s in range(2)]
+    theirs = [flux(matrix_y, [yrecv[s, j] for j in range(5)], yrecv[s, 5]) for s in range(2)]
+    mine = [flux(matrix_y, [ysend[s, j] for j in range(5)], ysend[s, 5]) for s in range(2)]
     odd = (lane & 1) == 1
     upper_pair = (lane & 2) == 2
     for i in range(5):
@@ -223,20 +232,29 @@
 
     def force(c):
         base = 8 + c * CHUNK
-
-        def plane(z, carry):
-            shift = (2 + 2 * LANES - 2 * CHUNK * c - 2 * z) & (LANES - 1)
+        part = pl.ds(c * CHUNK, CHUNK)
+        for z in range(depth):
+            shift = (2 - 2 * CHUNK * c - 2 * z) % LANES
             for i in range(5):
                 below2 = fx[i, z, base - 2 : base - 2 + CHUNK, :]
                 below1 = fx[i, z, base - 1 : base - 1 + CHUNK, :]
                 above1 = fx[i, z, base + 1 : base + 1 + CHUNK, :]
                 above2 = fx[i, z, base + 2 : base + 2 + CHUNK, :]
-                extra = jnp.where(edge, pltpu.roll(corr[z & 1, i], shift, 1), 0.0)
-                at = (i, z, pl.ds(c * CHUNK, CHUNK), slice(None))
-                w[at] = w[at] + extra + ((below2 - above2) + 8.0 * (above1 - below1))
-            return carry
-
-        lax.fori_loop(0, depth, plane, 0)
+                extra = corr[z % 2, i]
+                if shift:
+                    extra = pltpu.roll(extra, shift, 1)
+                extra = jnp.where(edge, extra, 0.0)
+                w[i, z, part, :] = (w[i, z, part, :] + extra) + ((below2 - above2) + 8.0 * (above1 - below1))
+
+    planes = min(4, depth)
+
+    def sweep(plane, carried):
+        def several(step, carried):
+            for u in range(planes):
+                carried = plane(step * planes + u, carried)
+            return carried
+
+        return lax.fori_loop(0, depth // planes, several, carried)
 
     def ahead(c):
         part = pl.ds(c * CHUNK, CHUNK)
@@ -259,7 +277,7 @@
                 result_here.append(total)
             return tuple(result_here)
 
-        carried = lax.fori_loop(0, depth, plane, tuple(up_recv[c, i] for i in range(5)))
+        carried = sweep(plane, tuple(up_recv[c, i] for i in range(5)))
         for i in range(5):
             up_send[c, i] = carried[i]
         pl.when(gz < nz - 1)(up_copy(c).start)
@@ -283,7 +301,7 @@
                 new.append(total)
             return tuple(new)
 
-        carried = lax.fori_loop(0, depth, plane, tuple(down_recv[c, i] for i in range(5)))
+        carried = sweep(plane, tuple(down_recv[c, i] for i in range(5)))
         for i in range(5):
             down_send[c, i] = carried[i]
         pl.when(gz > 0)(down_copy(c).start)
@@ -323,15 +341,21 @@
 def local(fields, metrics, jacobian_x, jacobian_y, pivot_inverse, lower_blocks, upper_blocks):
     _, depth, rows, columns = fields.shape
     chunks = rows // CHUNK
+    hbm = pl.BlockSpec(memory_space=pltpu.HBM)
     anywhere = pl.BlockSpec(memory_space=pl.ANY)
-    scalars = pl.BlockSpec(memory_space=pltpu.SMEM)
     dma = pltpu.SemaphoreType.DMA
+    arguments = [
+        pltpu.with_memory_space_constraint(argument, pltpu.HBM)
+        for argument in (fields, metrics, jacobian_x, jacobian_y, pivot_inverse, lower_blocks, upper_blocks)
+    ]
     return pl.pallas_call(
         kernel,
         out_shape=jax.ShapeDtypeStruct(fields.shape, F32),
-        in_specs=[anywhere, anywhere, scalars, scalars, anywhere, anywhere, anywhere],
+        in_specs=[hbm] * 7,
         out_specs=anywhere,
         scratch_shapes=[
+            pltpu.SMEM((5, 5), F32),
+            pltpu.SMEM((5, 5), F32),
             pltpu.VMEM((7, depth, rows, columns), F32),
             pltpu.VMEM(pivot_inverse.shape, BF16),
             pltpu.VMEM(pivot_inverse.shape, BF16),
@@ -349,6 +373,7 @@
             pltpu.VMEM((chunks, 5, CHUNK, LANES), F32),
             pltpu.VMEM((chunks, 5, CHUNK, LANES), F32),
             pltpu.VMEM((chunks, 5, CHUNK, LANES), F32),
+            dma((2,)),
             dma((7,)),
             dma((3, chunks)),
             dma((chunks,)),
@@ -360,9 +385,9 @@
             dma((chunks,)),
         ],
         compiler_params=pltpu.CompilerParams(
-            collective_id=0, has_side_effects=True, vmem_limit_bytes=48 * 1024 * 1024
+            collective_id=0, has_side_effects=True, vmem_limit_bytes=VMEM_LIMIT
         ),
-    )(fields, metrics, jacobian_x, jacobian_y, pivot_inverse, lower_blocks, upper_blocks)
+    )(*arguments)
 
 
 def solution(mesh):

time: 38.1 us -> 34.7 us (0.911)
  local copies, waits for them, and re-layouts: 4.09 us -> 1.49 us
  Pallas kernels: 33.8 us -> 33.1 us
    unnamed x7 -> x1, local copies, waits for them, and re-layouts: 4.09 us -> 1.49 us
    pallas_call x1, Pallas kernels: 33.8 us -> 33.1 us  [local(): pl.pallas_call(kernel, out_shape=jax.ShapeDtypeStruct(fields.shape, F32),...]
where the time goes in v2:
time: 34.7 us; the launch traced here: 34.6 us
  Pallas kernels  33.1 us (95%)
  local copies, waits for them, and re-layouts  1.49 us (4%)
    pallas_call x1, Pallas kernels, local(): pl.pallas_call(kernel, out_shape=jax.ShapeDtypeStruct(fields.shape, F32),...  33.1 us
    unnamed x1, local copies, waits for them, and re-layouts  1.49 us

profile of v2, /device:TPU:1, one launch (start us, length us, event | category | flops | bytes accessed | tf_op | source)
XLA Modules:
  0.0 34.6 jit_solution(190144715991177867)
XLA Ops:
  0.0 33.1 %shard_map.73 = f32[5,16,64,128]{3,2,1,0:T(8,128)S(1)} custom-call(f32[5,16,64,128]{3,2,1,0:T(8,128)} %fields.1, f32[2,16,64,128]{3,2,1,0:T(8,128)} %metrics.1, f32[5,5]{1,0:T(8,128)} %jacobian_x.1, f32[5,5]{1,0:T(8,128)} %jacobian_y.1, bf16[5,5,16,64,128]{4,3,2,1,0:T(8,128)(2,1)} %pivot.1, bf16[5,5,16,64,128]{4,3,2,1,0:T(8,128)(2,1)} %lower.1, ...), custom_call_target="tpu_custom_call" | custom-call | tf_op jit(solution)/shard_map/pallas_call | solution.py:351
  33.1 1.5 %copy.9 = f32[5,16,64,128]{3,2,1,0:T(8,128)} copy(f32[5,16,64,128]{3,2,1,0:T(8,128)S(1)} %shard_map.73) | data formatting | bytes 5242880

commit v3 on v2

--- a/solution.py
+++ b/solution.py
@@ -11,7 +11,7 @@
 LANES = 128
 F32 = jnp.float32
 BF16 = jnp.bfloat16
-VMEM_LIMIT = 48 * 1024 * 1024
+VMEM_LIMIT = 47 * 1024 * 1024
 
 
 def sum_of(terms):
@@ -23,23 +23,27 @@
 
 def kernel(
     fields, metrics, jacobian_x, jacobian_y, pivot, lower, upper, out,
-    jx, jy, cells, pv, lo, up, fx, w, result, band,
+    jx, jy, cells, pv, lo, up, product, fx, w, band,
     xsend, xrecv, ysend, yrecv, corr, up_send, up_recv, down_send, down_recv,
-    jacobian_sem, cell_sem, block_sem, out_sem, halo_ssem, halo_rsem, up_ssem, up_rsem, down_ssem, down_rsem,
+    jacobian_sem, cell_sem, block_sem, halo_ssem, halo_rsem, up_ssem, up_rsem, down_ssem, down_rsem,
 ):
     depth, rows = fields.shape[1], fields.shape[2]
     chunks = rows // CHUNK
+    order = (*range(1, chunks - 1), 0, chunks - 1)
     gx, gy, gz = lax.axis_index("gx"), lax.axis_index("gy"), lax.axis_index("gz")
     nx, ny, nz = lax.axis_size("gx"), lax.axis_size("gy"), lax.axis_size("gz")
 
-    cell_copies = [
+    cell_copies = []
+    for v in range(7):
+        source = fields.at[v] if v < 5 else metrics.at[v - 5]
+        cell_copies.append(pltpu.make_async_copy(source, cells.at[v], cell_sem.at[v]))
+    for v in (0, 1, 2, 3, 4, 6, 5):
+        cell_copies[v].start()
+    jacobian_copies = [
         pltpu.make_async_copy(jacobian_x, jx, jacobian_sem.at[0]),
         pltpu.make_async_copy(jacobian_y, jy, jacobian_sem.at[1]),
     ]
-    for v in range(7):
-        source = fields.at[v] if v < 5 else metrics.at[v - 5]
-        cell_copies.append(pltpu.make_async_copy(source, cells.at[v], cell_sem.at[v]))
-    for copy in cell_copies:
+    for copy in jacobian_copies:
         copy.start()
     block_copies = {}
     for kind, (source, target) in enumerate(((lower, lo), (pivot, pv), (upper, up))):
@@ -48,11 +52,6 @@
             block_copies[kind, c] = pltpu.make_async_copy(
                 source.at[:, :, :, part, :], target.at[:, :, :, part, :], block_sem.at[kind, c]
             )
-    for c in range(chunks):
-        block_copies[0, c].start()
-        block_copies[1, c].start()
-    for c in range(chunks):
-        block_copies[2, c].start()
 
     barrier = pltpu.get_barrier_semaphore()
     number = jnp.int32(0)
@@ -127,43 +126,46 @@
     weight = weight + jnp.where(d == LANES - 1, 8.0, 0.0) - jnp.where(d == 1, 8.0, 0.0)
     band[...] = weight.astype(BF16)
 
-    for copy in cell_copies:
-        copy.wait()
-
-    def pack_x(v, carry):
-        for z in range(depth):
-            xsend[0, v, 2 * z : 2 * z + 2, :] = cells[v, z, rows - 2 : rows, :]
-            xsend[1, v, 2 * z : 2 * z + 2, :] = cells[v, z, 0:2, :]
-        return carry
-
-    lax.fori_loop(0, 6, pack_x, 0)
-    pl.semaphore_wait(barrier, number)
-    for which in (0, 1):
-        copy, sends, _ = halos[which]
-        pl.when(sends)(copy.start)
-
     lane = lax.broadcasted_iota(jnp.int32, (CHUNK, LANES), 1)
     pair = lane >> 1
 
-    def pack_y(v, carry):
+    for v in range(6):
+        cell = v + v // 5
+        cell_copies[cell].wait()
         low = jnp.zeros((CHUNK, LANES), F32)
         high = low
         for c in range(chunks):
             for z in range(depth):
                 slot = CHUNK * c + z
-                rolled = cells[v + v // 5, z, c * CHUNK : (c + 1) * CHUNK, :]
+                rolled = cells[cell, z, c * CHUNK : (c + 1) * CHUNK, :]
                 if slot:
                     rolled = pltpu.roll(rolled, 2 * slot, 1)
                 low = jnp.where(pair == slot, rolled, low)
                 high = jnp.where(pair == (slot - 1) % (LANES // 2), rolled, high)
         ysend[0, v] = high
         ysend[1, v] = low
-        return carry
-
-    lax.fori_loop(0, 6, pack_y, 0)
+
+    pl.semaphore_wait(barrier, number)
     for which in (2, 3):
         copy, sends, _ = halos[which]
         pl.when(sends)(copy.start)
+    cell_copies[5].wait()
+    for c in order[: chunks // 2]:
+        block_copies[0, c].start()
+        block_copies[1, c].start()
+
+    def pack_x(v, carry):
+        for z in range(depth):
+            xsend[0, v, 2 * z : 2 * z + 2, :] = cells[v, z, rows - 2 : rows, :]
+            xsend[1, v, 2 * z : 2 * z + 2, :] = cells[v, z, 0:2, :]
+        return carry
+
+    lax.fori_loop(0, 6, pack_x, 0)
+    for which in (0, 1):
+        copy, sends, _ = halos[which]
+        pl.when(sends)(copy.start)
+    for copy in jacobian_copies:
+        copy.wait()
 
     matrix_x = [[jx[i, j] for j in range(5)] for i in range(5)]
     matrix_y = [[jy[i, j] for j in range(5)] for i in range(5)]
@@ -173,6 +175,9 @@
         return [factor * sum_of([matrix[i][j] * values[j] for j in range(5)]) for i in range(5)]
 
     def x_plane(z, carry):
+        for i in range(5):
+            fx[i, z, 0:8, :] = jnp.zeros((8, LANES), F32)
+            fx[i, z, rows + 8 : rows + 16, :] = jnp.zeros((8, LANES), F32)
         for c in range(chunks):
             part = pl.ds(c * CHUNK, CHUNK)
             values = flux(matrix_x, [cells[j, z, part, :] for j in range(5)], cells[5, z, part, :])
@@ -181,6 +186,9 @@
         return carry
 
     lax.fori_loop(0, depth, x_plane, 0)
+    for c in order[chunks // 2 :]:
+        block_copies[0, c].start()
+        block_copies[1, c].start()
 
     group = min(8, depth)
 
@@ -195,30 +203,32 @@
                     first = value.astype(BF16)
                     second = (value - first.astype(F32)).astype(BF16)
                     stacks.append(jnp.concatenate([first, second], 1))
-        product = jnp.dot(jnp.concatenate(stacks, 0), band[...], preferred_element_type=F32)
+        derived = jnp.dot(jnp.concatenate(stacks, 0), band[...], preferred_element_type=F32)
         for z in range(group):
             for c in range(chunks):
                 for i in range(5):
                     at = ((z * chunks + c) * 5 + i) * CHUNK
-                    w[i, step * group + z, c * CHUNK : (c + 1) * CHUNK, :] = product[at : at + CHUNK, :]
+                    plane = step * group + z
+                    base = 8 + c * CHUNK
+                    below2, below1, above1, above2 = (
+                        fx[i, plane, base + d : base + d + CHUNK, :] for d in (-2, -1, 1, 2)
+                    )
+                    along_x = (below2 - above2) + 8.0 * (above1 - below1)
+                    w[i, plane, c * CHUNK : (c + 1) * CHUNK, :] = derived[at : at + CHUNK, :] + along_x
         return carry
 
     lax.fori_loop(0, depth // group, y_planes, 0)
 
-    for copy, _, receives in halos:
-        pl.when(receives)(copy.wait_recv)
-
-    for side in range(2):
-        values = flux(matrix_x, [xrecv[side, j] for j in range(5)], xrecv[side, 5])
-        for i in range(5):
-            for z in range(depth):
-                start = 6 if side == 0 else 8 + rows
-                fx[i, z, start : start + 2, :] = values[i][2 * z : 2 * z + 2, :]
-
-    theirs = [flux(matrix_y, [yrecv[s, j] for j in range(5)], yrecv[s, 5]) for s in range(2)]
-    mine = [flux(matrix_y, [ysend[s, j] for j in range(5)], ysend[s, 5]) for s in range(2)]
+    for c in order:
+        block_copies[2, c].start()
+
     odd = (lane & 1) == 1
     upper_pair = (lane & 2) == 2
+    edge = (lane < 2) | (lane >= LANES - 2)
+    mine = [flux(matrix_y, [ysend[s, j] for j in range(5)], ysend[s, 5]) for s in range(2)]
+    for copy, _, receives in halos[2:]:
+        pl.when(receives)(copy.wait_recv)
+    theirs = [flux(matrix_y, [yrecv[s, j] for j in range(5)], yrecv[s, 5]) for s in range(2)]
     for i in range(5):
         high = theirs[0][i] - mine[0][i]
         low = theirs[1][i] - mine[1][i]
@@ -228,23 +238,20 @@
         corr[0, i] = jnp.where(upper_pair, at_start, at_end)
         corr[1, i] = jnp.where(upper_pair, at_end, at_start)
 
-    edge = (lane < 2) | (lane >= LANES - 2)
-
-    def force(c):
-        base = 8 + c * CHUNK
-        part = pl.ds(c * CHUNK, CHUNK)
-        for z in range(depth):
-            shift = (2 - 2 * CHUNK * c - 2 * z) % LANES
-            for i in range(5):
-                below2 = fx[i, z, base - 2 : base - 2 + CHUNK, :]
-                below1 = fx[i, z, base - 1 : base - 1 + CHUNK, :]
-                above1 = fx[i, z, base + 1 : base + 1 + CHUNK, :]
-                above2 = fx[i, z, base + 2 : base + 2 + CHUNK, :]
-                extra = corr[z % 2, i]
-                if shift:
-                    extra = pltpu.roll(extra, shift, 1)
-                extra = jnp.where(edge, extra, 0.0)
-                w[i, z, part, :] = (w[i, z, part, :] + extra) + ((below2 - above2) + 8.0 * (above1 - below1))
+    def add_x_halo(side):
+        copy, _, receives = halos[side]
+        pl.when(receives)(copy.wait_recv)
+        values = flux(matrix_x, [xrecv[side, j] for j in range(5)], xrecv[side, 5])
+        odd_row = (lax.broadcasted_iota(jnp.int32, (2 * depth, LANES), 0) & 1) == 1
+        for i in range(5):
+            if side == 0:
+                extra = values[i] - jnp.where(odd_row, 0.0, 8.0 * pltpu.roll(values[i], 2 * depth - 1, 0))
+                start = 0
+            else:
+                extra = jnp.where(odd_row, 8.0 * pltpu.roll(values[i], 1, 0), 0.0) - values[i]
+                start = rows - 2
+            for z in range(depth):
+                w[i, z, start : start + 2, :] = w[i, z, start : start + 2, :] + extra[2 * z : 2 * z + 2, :]
 
     planes = min(4, depth)
 
@@ -265,8 +272,12 @@
 
         def plane(z, carried):
             inner = []
-            for i in range(5):
-                total = w[i, z, part, :]
+            shift = (2 - 2 * CHUNK * c - 2 * z) % LANES
+            for i in range(5):
+                extra = corr[z % 2, i]
+                if shift:
+                    extra = pltpu.roll(extra, shift, 1)
+                total = w[i, z, part, :] + jnp.where(edge, extra, 0.0)
                 for j in range(5):
                     total = total - lo[i, j, z, part, :].astype(F32) * carried[j]
                 inner.append(total)
@@ -277,14 +288,54 @@
                 result_here.append(total)
             return tuple(result_here)
 
-        carried = sweep(plane, tuple(up_recv[c, i] for i in range(5)))
+        carried = tuple(up_recv[c, i] for i in range(5))
+        for z in range(depth):
+            carried = plane(z, carried)
         for i in range(5):
             up_send[c, i] = carried[i]
         pl.when(gz < nz - 1)(up_copy(c).start)
 
-    def out_copy(c):
+    def prepare(c):
         part = pl.ds(c * CHUNK, CHUNK)
-        return pltpu.make_async_copy(result.at[:, :, part, :], out.at[:, :, part, :], out_sem.at[c])
+        block_copies[0, c].wait()
+        block_copies[1, c].wait()
+        for z in range(depth):
+            shift = (2 - 2 * CHUNK * c - 2 * z) % LANES
+            source = []
+            for i in range(5):
+                extra = corr[z % 2, i]
+                if shift:
+                    extra = pltpu.roll(extra, shift, 1)
+                source.append(w[i, z, part, :] + jnp.where(edge, extra, 0.0))
+            for i in range(5):
+                w[i, z, part, :] = sum_of([pv[i, j, z, part, :].astype(F32) * source[j] for j in range(5)])
+
+        def plane(z, carry):
+            for j in range(5):
+                column = [lo[k, j, z, part, :].astype(F32) for k in range(5)]
+                for i in range(5):
+                    product[i, j, z, part, :] = sum_of(
+                        [pv[i, k, z, part, :].astype(F32) * column[k] for k in range(5)]
+                    )
+            return carry
+
+        lax.fori_loop(0, depth, plane, 0)
+
+    def ahead_prepared(c):
+        part = pl.ds(c * CHUNK, CHUNK)
+        up_copy(c).wait_recv()
+
+        def plane(z, carried):
+            new = []
+            for i in range(5):
+                total = w[i, z, part, :]
+                for j in range(5):
+                    total = total - product[i, j, z, part, :] * carried[j]
+                w[i, z, part, :] = total
+                new.append(total)
+            return tuple(new)
+
+        sweep(plane, tuple(up_recv[c, i] for i in range(5)))
 
     def back(c):
         part = pl.ds(c * CHUNK, CHUNK)
@@ -297,7 +348,7 @@
                 total = w[i, z, part, :]
                 for j in range(5):
                     total = total - up[i, j, z, part, :].astype(F32) * carried[j]
-                result[i, z, part, :] = cells[i, z, part, :] + total
+                out[i, z, part, :] = cells[i, z, part, :] + total
                 new.append(total)
             return tuple(new)
 
@@ -305,33 +356,31 @@
         for i in range(5):
             down_send[c, i] = carried[i]
         pl.when(gz > 0)(down_copy(c).start)
-        out_copy(c).start()
-
-    @pl.when(gz > 0)
-    def _():
-        for c in range(chunks):
-            force(c)
-
-    for c in range(chunks):
-        @pl.when(gz == 0)
-        def _():
-            force(c)
-
-        ahead(c)
-
-        @pl.when(gz == nz - 1)
-        def _():
+
+    @pl.when(gz < nz - 1)
+    def _():
+        for c in order:
+            if c == 0:
+                add_x_halo(0)
+            if c == chunks - 1:
+                add_x_halo(1)
+            ahead(c)
+        for c in order:
             block_copies[2, c].wait()
             back(c)
 
-    @pl.when(gz < nz - 1)
-    def _():
-        for c in range(chunks):
+    @pl.when(gz == nz - 1)
+    def _():
+        add_x_halo(0)
+        add_x_halo(1)
+        for c in order:
+            prepare(c)
+        for c in order:
+            ahead_prepared(c)
             block_copies[2, c].wait()
             back(c)
 
     for c in range(chunks):
-        out_copy(c).wait()
         pl.when(gz < nz - 1)(up_copy(c).wait_send)
         pl.when(gz > 0)(down_copy(c).wait_send)
     for copy, sends, _ in halos:
@@ -352,7 +401,7 @@
         kernel,
         out_shape=jax.ShapeDtypeStruct(fields.shape, F32),
         in_specs=[hbm] * 7,
-        out_specs=anywhere,
+        out_specs=pl.BlockSpec(memory_space=pltpu.VMEM),
         scratch_shapes=[
             pltpu.SMEM((5, 5), F32),
             pltpu.SMEM((5, 5), F32),
@@ -360,8 +409,8 @@
             pltpu.VMEM(pivot_inverse.shape, BF16),
             pltpu.VMEM(pivot_inverse.shape, BF16),
             pltpu.VMEM(pivot_inverse.shape, BF16),
+            pltpu.VMEM(pivot_inverse.shape, F32),
             pltpu.VMEM((5, depth, rows + 16, columns), F32),
-            pltpu.VMEM(fields.shape, F32),
             pltpu.VMEM(fields.shape, F32),
             pltpu.VMEM((2 * LANES, LANES), BF16),
             pltpu.VMEM((2, 6, 2 * depth, columns), F32),
@@ -376,7 +425,6 @@
             dma((2,)),
             dma((7,)),
             dma((3, chunks)),
-            dma((chunks,)),
             dma((4,)),
             dma((4,)),
             dma((chunks,)),

time: 34.7 us -> 26.5 us (0.76)
  Pallas kernels: 33.1 us -> 24.9 us
    pallas_call x1, Pallas kernels: 33.1 us -> 24.9 us  [local(): pl.pallas_call(kernel, out_shape=jax.ShapeDtypeStruct(fields.shape, F32),...]
where the time goes in v3:
time: 26.5 us; the launch traced here: 26.4 us
  Pallas kernels  24.9 us (94%)
  local copies, waits for them, and re-layouts  1.49 us (6%)
    pallas_call x1, Pallas kernels, local(): pl.pallas_call(kernel, out_shape=jax.ShapeDtypeStruct(fields.shape, F32),...  24.9 us
    unnamed x1, local copies, waits for them, and re-layouts  1.49 us

profile of v3, /device:TPU:1, one launch (start us, length us, event | category | flops | bytes accessed | tf_op | source)
XLA Modules:
  0.0 26.4 jit_solution(3302266110103250559)
XLA Ops:
  0.0 24.9 %shard_map.73 = f32[5,16,64,128]{3,2,1,0:T(8,128)S(1)} custom-call(f32[5,16,64,128]{3,2,1,0:T(8,128)} %fields.1, f32[2,16,64,128]{3,2,1,0:T(8,128)} %metrics.1, f32[5,5]{1,0:T(8,128)} %jacobian_x.1, f32[5,5]{1,0:T(8,128)} %jacobian_y.1, bf16[5,5,16,64,128]{4,3,2,1,0:T(8,128)(2,1)} %pivot.1, bf16[5,5,16,64,128]{4,3,2,1,0:T(8,128)(2,1)} %lower.1, ...), custom_call_target="tpu_custom_call" | custom-call | tf_op jit(solution)/shard_map/pallas_call | solution.py:400
  24.9 1.5 %copy.9 = f32[5,16,64,128]{3,2,1,0:T(8,128)} copy(f32[5,16,64,128]{3,2,1,0:T(8,128)S(1)} %shard_map.73) | data formatting | bytes 5242880

commit v4 on v3

--- a/solution.py
+++ b/solution.py
@@ -29,9 +29,22 @@
 ):
     depth, rows = fields.shape[1], fields.shape[2]
     chunks = rows // CHUNK
-    order = (*range(1, chunks - 1), 0, chunks - 1)
+    order = (*range(1, chunks), 0)
     gx, gy, gz = lax.axis_index("gx"), lax.axis_index("gy"), lax.axis_index("gz")
     nx, ny, nz = lax.axis_size("gx"), lax.axis_size("gy"), lax.axis_size("gz")
+
+    barrier = pltpu.get_barrier_semaphore()
+    number = jnp.int32(0)
+    for axis, place, size in (("gx", gx, nx), ("gy", gy, ny), ("gz", gz, nz)):
+        @pl.when(place > 0)
+        def _():
+            pl.semaphore_signal(barrier, inc=1, device_id={axis: place - 1}, device_id_type=pl.DeviceIdType.MESH)
+
+        @pl.when(place < size - 1)
+        def _():
+            pl.semaphore_signal(barrier, inc=1, device_id={axis: place + 1}, device_id_type=pl.DeviceIdType.MESH)
+
+        number = number + jnp.where(place > 0, 1, 0) + jnp.where(place < size - 1, 1, 0)
 
     cell_copies = []
     for v in range(7):
@@ -45,26 +58,12 @@
     ]
     for copy in jacobian_copies:
         copy.start()
-    block_copies = {}
-    for kind, (source, target) in enumerate(((lower, lo), (pivot, pv), (upper, up))):
-        for c in range(chunks):
-            part = pl.ds(c * CHUNK, CHUNK)
-            block_copies[kind, c] = pltpu.make_async_copy(
-                source.at[:, :, :, part, :], target.at[:, :, :, part, :], block_sem.at[kind, c]
-            )
-
-    barrier = pltpu.get_barrier_semaphore()
-    number = jnp.int32(0)
-    for axis, place, size in (("gx", gx, nx), ("gy", gy, ny), ("gz", gz, nz)):
-        @pl.when(place > 0)
-        def _():
-            pl.semaphore_signal(barrier, inc=1, device_id={axis: place - 1}, device_id_type=pl.DeviceIdType.MESH)
-
-        @pl.when(place < size - 1)
-        def _():
-            pl.semaphore_signal(barrier, inc=1, device_id={axis: place + 1}, device_id_type=pl.DeviceIdType.MESH)
-
-        number = number + jnp.where(place > 0, 1, 0) + jnp.where(place < size - 1, 1, 0)
+    def block_copy(kind, c):
+        part = pl.ds(c * CHUNK if isinstance(c, int) else pl.multiple_of(c * CHUNK, CHUNK), CHUNK)
+        source, target = ((lower, lo), (pivot, pv), (upper, up))[kind]
+        return pltpu.make_async_copy(
+            source.at[:, :, :, part, :], target.at[:, :, :, part, :], block_sem.at[kind, c]
+        )
 
     def halo_copy(which, target):
         source, destination = ((xsend, xrecv), (ysend, yrecv))[which // 2]
@@ -129,9 +128,7 @@
     lane = lax.broadcasted_iota(jnp.int32, (CHUNK, LANES), 1)
     pair = lane >> 1
 
-    for v in range(6):
-        cell = v + v // 5
-        cell_copies[cell].wait()
+    def pack_y(v, cell):
         low = jnp.zeros((CHUNK, LANES), F32)
         high = low
         for c in range(chunks):
@@ -145,14 +142,23 @@
         ysend[0, v] = high
         ysend[1, v] = low
 
+    def pack_field(v, carry):
+        pltpu.make_async_copy(fields.at[v], cells.at[v], cell_sem.at[v]).wait()
+        pack_y(v, v)
+        return carry
+
+    lax.fori_loop(0, 5, pack_field, 0)
+    cell_copies[6].wait()
+    pack_y(5, 6)
+
     pl.semaphore_wait(barrier, number)
     for which in (2, 3):
         copy, sends, _ = halos[which]
         pl.when(sends)(copy.start)
     cell_copies[5].wait()
     for c in order[: chunks // 2]:
-        block_copies[0, c].start()
-        block_copies[1, c].start()
+        block_copy(0, c).start()
+        block_copy(1, c).start()
 
     def pack_x(v, carry):
         for z in range(depth):
@@ -187,8 +193,8 @@
 
     lax.fori_loop(0, depth, x_plane, 0)
     for c in order[chunks // 2 :]:
-        block_copies[0, c].start()
-        block_copies[1, c].start()
+        block_copy(0, c).start()
+        block_copy(1, c).start()
 
     group = min(8, depth)
 
@@ -220,7 +226,36 @@
     lax.fori_loop(0, depth // group, y_planes, 0)
 
     for c in order:
-        block_copies[2, c].start()
+        block_copy(2, c).start()
+
+    def each_chunk(body):
+        def step(k, carry):
+            body(lax.rem(k + 1, chunks))
+            return carry
+
+        lax.fori_loop(0, chunks, step, 0)
+
+    def multiply(c):
+        part = pl.ds(pl.multiple_of(c * CHUNK, CHUNK), CHUNK)
+        block_copy(0, c).wait()
+        block_copy(1, c).wait()
+
+        def plane(z, carry):
+            for j in range(5):
+                column = [lo[k, j, z, part, :].astype(F32) for k in range(5)]
+                for i in range(5):
+                    product[i, j, z, part, :] = sum_of(
+                        [pv[i, k, z, part, :].astype(F32) * column[k] for k in range(5)]
+                    )
+            return carry
+
+        lax.fori_loop(0, depth, plane, 0)
+
+    prepares = max(nz - 2, 1)
+
+    @pl.when(gz >= prepares)
+    def _():
+        each_chunk(multiply)
 
     odd = (lane & 1) == 1
     upper_pair = (lane & 2) == 2
@@ -235,8 +270,9 @@
         at_start = high - jnp.where(odd, 0.0, 8.0 * pltpu.roll(high, LANES - 1, 1))
         at_end = jnp.where(odd, 8.0 * pltpu.roll(low, 1, 1), 0.0) - low
         at_end = pltpu.roll(at_end, LANES - 4, 1)
-        corr[0, i] = jnp.where(upper_pair, at_start, at_end)
-        corr[1, i] = jnp.where(upper_pair, at_end, at_start)
+        first = (2 - 2 * CHUNK * order[0]) % LANES
+        corr[0, i] = pltpu.roll(jnp.where(upper_pair, at_start, at_end), first, 1)
+        corr[1, i] = pltpu.roll(jnp.where(upper_pair, at_end, at_start), (first - 2) % LANES, 1)
 
     def add_x_halo(side):
         copy, _, receives = halos[side]
@@ -253,79 +289,76 @@
             for z in range(depth):
                 w[i, z, start : start + 2, :] = w[i, z, start : start + 2, :] + extra[2 * z : 2 * z + 2, :]
 
-    planes = min(4, depth)
+    planes = min(8, depth)
+
+    def forcing(z, u, part):
+        source = []
+        for i in range(5):
+            extra = corr[u % 2, i]
+            corr[u % 2, i] = pltpu.roll(extra, LANES - 4, 1)
+            source.append(w[i, z, part, :] + jnp.where(edge, extra, 0.0))
+        return source
+
+    def next_chunk():
+        turn = (2 * depth - 2 * CHUNK) % LANES
+        if turn:
+            for p in range(2):
+                for i in range(5):
+                    corr[p, i] = pltpu.roll(corr[p, i], turn, 1)
 
     def sweep(plane, carried):
         def several(step, carried):
             for u in range(planes):
-                carried = plane(step * planes + u, carried)
+                carried = plane(step * planes + u, u, carried)
             return carried
 
         return lax.fori_loop(0, depth // planes, several, carried)
 
     def ahead(c):
-        part = pl.ds(c * CHUNK, CHUNK)
-        block_copies[0, c].wait()
-        block_copies[1, c].wait()
+        part = pl.ds(pl.multiple_of(c * CHUNK, CHUNK), CHUNK)
+        block_copy(0, c).wait()
+        block_copy(1, c).wait()
 
         pl.when(gz > 0)(up_copy(c).wait_recv)
 
-        def plane(z, carried):
+        def plane(z, u, carried):
+            source = forcing(z, u, part)
             inner = []
-            shift = (2 - 2 * CHUNK * c - 2 * z) % LANES
-            for i in range(5):
-                extra = corr[z % 2, i]
-                if shift:
-                    extra = pltpu.roll(extra, shift, 1)
-                total = w[i, z, part, :] + jnp.where(edge, extra, 0.0)
+            for i in range(5):
+                total = source[i]
                 for j in range(5):
                     total = total - lo[i, j, z, part, :].astype(F32) * carried[j]
                 inner.append(total)
-            result_here = []
+            new = []
             for i in range(5):
                 total = sum_of([pv[i, j, z, part, :].astype(F32) * inner[j] for j in range(5)])
                 w[i, z, part, :] = total
-                result_here.append(total)
-            return tuple(result_here)
-
-        carried = tuple(up_recv[c, i] for i in range(5))
-        for z in range(depth):
-            carried = plane(z, carried)
+                new.append(total)
+            return tuple(new)
+
+        carried = sweep(plane, tuple(up_recv[c, i] for i in range(5)))
         for i in range(5):
             up_send[c, i] = carried[i]
         pl.when(gz < nz - 1)(up_copy(c).start)
+        next_chunk()
 
     def prepare(c):
-        part = pl.ds(c * CHUNK, CHUNK)
-        block_copies[0, c].wait()
-        block_copies[1, c].wait()
-        for z in range(depth):
-            shift = (2 - 2 * CHUNK * c - 2 * z) % LANES
-            source = []
-            for i in range(5):
-                extra = corr[z % 2, i]
-                if shift:
-                    extra = pltpu.roll(extra, shift, 1)
-                source.append(w[i, z, part, :] + jnp.where(edge, extra, 0.0))
+        part = pl.ds(pl.multiple_of(c * CHUNK, CHUNK), CHUNK)
+
+        def scale(z, u, carry):
+            source = forcing(z, u, part)
             for i in range(5):
                 w[i, z, part, :] = sum_of([pv[i, j, z, part, :].astype(F32) * source[j] for j in range(5)])
-
-        def plane(z, carry):
-            for j in range(5):
-                column = [lo[k, j, z, part, :].astype(F32) for k in range(5)]
-                for i in range(5):
-                    product[i, j, z, part, :] = sum_of(
-                        [pv[i, k, z, part, :].astype(F32) * column[k] for k in range(5)]
-                    )
             return carry
 
-        lax.fori_loop(0, depth, plane, 0)
+        sweep(scale, 0)
+        next_chunk()
 
     def ahead_prepared(c):
-        part = pl.ds(c * CHUNK, CHUNK)
+        part = pl.ds(pl.multiple_of(c * CHUNK, CHUNK), CHUNK)
         up_copy(c).wait_recv()
 
-        def plane(z, carried):
+        def plane(z, u, carried):
             new = []
             for i in range(5):
                 total = w[i, z, part, :]
@@ -335,13 +368,16 @@
                 new.append(total)
             return tuple(new)
 
-        sweep(plane, tuple(up_recv[c, i] for i in range(5)))
+        carried = sweep(plane, tuple(up_recv[c, i] for i in range(5)))
+        for i in range(5):
+            up_send[c, i] = carried[i]
+        pl.when(gz < nz - 1)(up_copy(c).start)
 
     def back(c):
-        part = pl.ds(c * CHUNK, CHUNK)
+        part = pl.ds(pl.multiple_of(c * CHUNK, CHUNK), CHUNK)
         pl.when(gz < nz - 1)(down_copy(c).wait_recv)
 
-        def plane(step, carried):
+        def plane(step, u, carried):
             z = depth - 1 - step
             new = []
             for i in range(5):
@@ -357,28 +393,43 @@
             down_send[c, i] = carried[i]
         pl.when(gz > 0)(down_copy(c).start)
 
-    @pl.when(gz < nz - 1)
-    def _():
-        for c in order:
-            if c == 0:
+    @pl.when(gz < prepares)
+    def _():
+        def forward(c):
+            @pl.when(c == chunks - 1)
+            def _():
+                add_x_halo(1)
+
+            @pl.when(c == 0)
+            def _():
                 add_x_halo(0)
-            if c == chunks - 1:
-                add_x_halo(1)
+
             ahead(c)
-        for c in order:
-            block_copies[2, c].wait()
-            back(c)
-
-    @pl.when(gz == nz - 1)
-    def _():
+
+        each_chunk(forward)
+
+    @pl.when(gz >= prepares)
+    def _():
+        def both(c):
+            ahead_prepared(c)
+
+            @pl.when(gz == nz - 1)
+            def _():
+                block_copy(2, c).wait()
+                back(c)
+
         add_x_halo(0)
         add_x_halo(1)
-        for c in order:
-            prepare(c)
-        for c in order:
-            ahead_prepared(c)
-            block_copies[2, c].wait()
+        each_chunk(prepare)
+        each_chunk(both)
+
+    @pl.when(gz < nz - 1)
+    def _():
+        def backward(c):
+            block_copy(2, c).wait()
             back(c)
+
+        each_chunk(backward)
 
     for c in range(chunks):
         pl.when(gz < nz - 1)(up_copy(c).wait_send)

time: 26.5 us -> 25.9 us (0.977)
  Pallas kernels: 24.9 us -> 24.3 us
    pallas_call x1, Pallas kernels: 24.9 us -> 24.3 us  [local(): pl.pallas_call(kernel, out_shape=jax.ShapeDtypeStruct(fields.shape, F32),...]
where the time goes in v4:
time: 25.9 us; the launch traced here: 25.8 us
  Pallas kernels  24.3 us (94%)
  local copies, waits for them, and re-layouts  1.49 us (6%)
    pallas_call x1, Pallas kernels, local(): pl.pallas_call(kernel, out_shape=jax.ShapeDtypeStruct(fields.shape, F32),...  24.3 us
    unnamed x1, local copies, waits for them, and re-layouts  1.49 us

profile of v4, /device:TPU:1, one launch (start us, length us, event | category | flops | bytes accessed | tf_op | source)
XLA Modules:
  0.0 25.8 jit_solution(6696190752348099107)
XLA Ops:
  0.0 24.3 %shard_map.73 = f32[5,16,64,128]{3,2,1,0:T(8,128)S(1)} custom-call(f32[5,16,64,128]{3,2,1,0:T(8,128)} %fields.1, f32[2,16,64,128]{3,2,1,0:T(8,128)} %metrics.1, f32[5,5]{1,0:T(8,128)} %jacobian_x.1, f32[5,5]{1,0:T(8,128)} %jacobian_y.1, bf16[5,5,16,64,128]{4,3,2,1,0:T(8,128)(2,1)} %pivot.1, bf16[5,5,16,64,128]{4,3,2,1,0:T(8,128)(2,1)} %lower.1, ...), custom_call_target="tpu_custom_call" | custom-call | tf_op jit(solution)/shard_map/pallas_call | solution.py:451
  24.3 1.5 %copy.9 = f32[5,16,64,128]{3,2,1,0:T(8,128)} copy(f32[5,16,64,128]{3,2,1,0:T(8,128)S(1)} %shard_map.73) | data formatting | bytes 5242880
